TPU v7x, 32 devices: a whole 2x2x4 slice. The times are simulated.
32 devices in a mesh: seg: 16 (over z, y, x), samp: 2 (over core).
Axes of the slice: x: 2, y: 2, z: 4, core: 2. Of those that a mesh axis runs over, the one named last changes fastest.
Arguments:
- rigidity_diagonal_cells: bfloat16 [512, 128, 128], P('seg')
- rigidity_lower_cells: bfloat16 [512, 128, 128], P('seg'), may hold values from -0.5 to 0.5
- inverse_diagonal_cells: bfloat16 [512, 128, 128], P('seg')
- bedding_rigidity_per_unknown: float32 [512, 128], P('seg'), may hold values from 0.3 to 2
- bedding_regime: int32 [512], P('seg'), may hold values from 0 to 2
- dilation_push_per_kelvin: float32 [512, 128], P('seg'), may hold values from 1 to 16
- heat_shape_functions: bfloat16 [512, 512], P('seg'), may hold values from -0.25 to 0.25
- sampled_shape_weights: bfloat16 [64, 512], P('samp'), may hold values from -6 to 6
- joined_segment_table: int32 [16, 2], P('seg'), may hold values from 0 to 15
- joint_rigidity: float32 [16, 2], P('seg'), may hold values from 1.2 to 3.6
Outputs:
- displacement: float32 [64, 512, 128], P('samp', 'seg')
- kl_grad: float32 [512], replicated
Inputs may be any that keep to these rules, and one draw needn't show every extreme that they name: `joined_segment_table`: every entry names a segment.
All inputs are finite; a program needn't handle non-finite values.
Results may differ from a plain program's by a relative error of at most 0.013.
Values may be sent and summed in bfloat16 or wider, within the bound.
A program may use at most 64 MiB of HBM per device.

v0:
```python
import math
import jax
import jax.numpy as jnp
from jax import lax
from jax.sharding import PartitionSpec as P

STEPS = 4


def shifted(value, axis, steps):
    count = lax.axis_size(axis)
    first, last = (max(0, -steps), min(count, count - steps))
    return lax.ppermute(value, axis, [(source, source + steps) for source in range(first, last)])


def stiffness(
    field_round, rigidity_diagonal_cells, rigidity_lower_cells, joined_segment_table, joint_rigidity
):
    own_term = jnp.einsum(
        "sjb,jab->sja", field_round, rigidity_diagonal_cells, preferred_element_type=jnp.float32
    )
    upward = jnp.einsum(
        "sjb,jba->sja", field_round, rigidity_lower_cells, preferred_element_type=jnp.float32
    ).astype(jnp.bfloat16)
    below_rim = shifted(field_round[:, -1:, :], "seg", 1)
    above_rim = shifted(upward[:, :1, :], "seg", -1)
    interfaces = lax.all_gather(field_round[:, :1, :], "seg", axis=1, tiled=True)
    lower_field = jnp.concatenate([below_rim, field_round[:, :-1]], axis=1)
    below_term = jnp.einsum(
        "sjb,jab->sja", lower_field, rigidity_lower_cells, preferred_element_type=jnp.float32
    )
    upper_term = jnp.concatenate([upward[:, 1:], above_rim], axis=1).astype(jnp.float32)
    result = own_term + below_term + upper_term
    partner = jnp.take(interfaces, joined_segment_table[0], axis=1).astype(jnp.float32)
    own_interface = field_round[:, 0:1, :].astype(jnp.float32)
    spring = jnp.sum(joint_rigidity[0][None, :, None] * (own_interface - partner), axis=1)
    return result.at[:, 0, :].add(spring)


def ballast(state, bedding_rigidity_per_unknown, bedding_regime):
    code = bedding_regime[None, :, None]
    stiff = bedding_rigidity_per_unknown[None]
    magnitude = 1.0 + jnp.abs(state)
    slide = jnp.tanh(state)
    force = jnp.where(
        code == 0, stiff * state, jnp.where(code == 1, stiff * state / magnitude, stiff * slide)
    )
    tangent = jnp.where(
        code == 0,
        stiff + 0.0 * state,
        jnp.where(code == 1, stiff / (magnitude * magnitude), stiff * (1.0 - slide * slide)),
    )
    return (force, tangent)


def blockwise(inverse_diagonal_cells, field_round):
    return jnp.einsum(
        "jab,sjb->sja", inverse_diagonal_cells, field_round, preferred_element_type=jnp.float32
    )


def body(
    rigidity_diagonal_cells,
    rigidity_lower_cells,
    inverse_diagonal_cells,
    bedding_rigidity_per_unknown,
    bedding_regime,
    dilation_push_per_kelvin,
    heat_shape_functions,
    sampled_shape_weights,
    joined_segment_table,
    joint_rigidity,
):
    samples_here = sampled_shape_weights.shape[0]
    blocks_here = rigidity_diagonal_cells.shape[0]
    width = rigidity_diagonal_cells.shape[1]
    shape_functions = heat_shape_functions.shape[1]
    complete_shape_functions = heat_shape_functions.astype(jnp.float32)
    heat_distribution = jnp.dot(
        sampled_shape_weights, heat_shape_functions.T, preferred_element_type=jnp.float32
    )
    heat_driven_source = dilation_push_per_kelvin[None] * heat_distribution[:, :, None]
    state = jnp.zeros((samples_here, blocks_here, width), jnp.float32)
    grad_total = jnp.zeros((shape_functions,), jnp.float32)
    for iteration in range(STEPS):
        state_round = state.astype(jnp.bfloat16)
        force, tangent = ballast(state, bedding_rigidity_per_unknown, bedding_regime)
        residual_vector = (
            heat_driven_source
            - stiffness(
                state_round,
                rigidity_diagonal_cells,
                rigidity_lower_cells,
                joined_segment_table,
                joint_rigidity,
            )
            - force
        )
        initial_newton_step = blockwise(
            inverse_diagonal_cells, residual_vector.astype(jnp.bfloat16)
        )
        second = (
            residual_vector
            - stiffness(
                initial_newton_step.astype(jnp.bfloat16),
                rigidity_diagonal_cells,
                rigidity_lower_cells,
                joined_segment_table,
                joint_rigidity,
            )
            - tangent * initial_newton_step
        )
        state = (
            state
            + initial_newton_step
            + blockwise(inverse_diagonal_cells, second.astype(jnp.bfloat16))
        )
        adjoint = jnp.einsum(
            "sja,jab->sjb",
            state.astype(jnp.bfloat16),
            inverse_diagonal_cells,
            preferred_element_type=jnp.float32,
        )
        weighted = jnp.sum(jnp.sum(dilation_push_per_kelvin[None] * adjoint, axis=2), axis=0)
        partial_value = jnp.dot(weighted, complete_shape_functions, precision=lax.Precision.HIGHEST)
        grad_total = grad_total + lax.psum(partial_value, ("seg", "samp"))
    every_block_list = blocks_here * lax.axis_size("seg")
    all_samples = samples_here * lax.axis_size("samp")
    scale = math.sqrt(shape_functions / (every_block_list * all_samples * width))
    return (state, grad_total * scale)


def solution(mesh):
    placed = (
        P("seg", None, None),
        P("seg", None, None),
        P("seg", None, None),
        P("seg", None),
        P("seg"),
        P("seg", None),
        P("seg", None),
        P("samp", None),
        P("seg", None),
        P("seg", None),
    )
    return jax.shard_map(
        body, mesh=mesh, in_specs=placed, out_specs=(P("samp", "seg", None), P()), check_vma=False
    )
```

profile of v0, /device:TPU:14, one launch (start us, length us, event | category | flops | bytes accessed | tf_op | source)
XLA Modules:
  0.0 460.8 jit_solution(1154479130879753834)
XLA Ops:
  0.7 3.5 collective-permute-start
  4.6 2.6 collective-permute-start.1
  8.5 1.5 fusion.94
  16.1 1.5 fusion.140
  17.6 4.8 %collective-permute-start.2 = (bf16[32,1,128]{2,0,1:T(8,128)(2,1)}, bf16[32,1,128]{2,0,1:T(8,128)(2,1)}, u32[]{:S(2)}, u32[]{:S(2)}) collective-permute-start(bf16[32,1,128]{2,0,1:T(8,128)(2,1)} %get-tuple-element.125), channel_id=1, source_target_pairs={{0,2},{2,4},{4,6},{6,8},{8,10},{10,12},{12,14},{14,16},{16,18},{18... | collective-permute-start | bytes 24584 | tf_op jit(solution)/shard_map/ppermute | solution.py:13
  22.4 30.9 %all_gather.22 = bf16[32,16,128]{2,0,1:T(8,128)(2,1)} all-gather(bf16[32,1,128]{2,0,1:T(8,128)(2,1)S(1)} %get-tuple-element.124), channel_id=1, replica_groups=mesh['seg'=16,'samp'=2] {'seg'}, dimensions={1}, use_global_device_ids=true | all-gather | bytes 139264 | tf_op jit(solution)/shard_map/all_gather | solution.py:27
  53.3 1.5 gather_fusion.1
  55.5 3.5 collective-permute-start.3
  59.1 4.1 collective-permute-done.3
  64.6 1.5 fusion.133
  68.3 1.5 fusion.141
  69.9 3.9 collective-permute-start.4
  73.8 34.6 %all_gather.23 = bf16[32,16,128]{2,0,1:T(8,128)(2,1)} all-gather(bf16[32,1,128]{2,0,1:T(8,128)(2,1)S(1)} %get-tuple-element.121), channel_id=1, replica_groups=mesh['seg'=16,'samp'=2] {'seg'}, dimensions={1}, use_global_device_ids=true | all-gather | bytes 139264 | tf_op jit(solution)/shard_map/all_gather | solution.py:27
  108.4 1.5 gather_fusion.2
  110.5 1.9 collective-permute-start.5
  112.6 5.3 %collective-permute-done.5 = bf16[32,1,128]{2,0,1:T(8,128)(2,1)S(1)} collective-permute-done((bf16[32,1,128]{2,0,1:T(8,128)(2,1)S(1)}, bf16[32,1,128]{2,0,1:T(8,128)(2,1)S(1)}, u32[]{:S(2)}, u32[]{:S(2)}) %collective-permute-start.5) | collective-permute-done | bytes 8224 | tf_op jit(solution)/shard_map/ppermute | solution.py:13
  119.9 1.5 fusion.134
  124.6 1.9 collective-permute-start.6
  126.5 40.1 %all_gather.24 = bf16[32,16,128]{2,0,1:T(8,128)(2,1)} all-gather(bf16[32,1,128]{2,0,1:T(8,128)(2,1)S(1)} %get-tuple-element.118), channel_id=1, replica_groups=mesh['seg'=16,'samp'=2] {'seg'}, dimensions={1}, use_global_device_ids=true | all-gather | bytes 139264 | tf_op jit(solution)/shard_map/all_gather | solution.py:27
  166.6 1.5 gather_fusion.3
  168.8 1.9 collective-permute-start.7
  170.9 5.2 %collective-permute-done.7 = bf16[32,1,128]{2,0,1:T(8,128)(2,1)S(1)} collective-permute-done((bf16[32,1,128]{2,0,1:T(8,128)(2,1)S(1)}, bf16[32,1,128]{2,0,1:T(8,128)(2,1)S(1)}, u32[]{:S(2)}, u32[]{:S(2)}) %collective-permute-start.7) | collective-permute-done | bytes 8224 | tf_op jit(solution)/shard_map/ppermute | solution.py:13
  178.2 1.6 fusion.135
  181.9 1.5 fusion.143
  184.1 1.9 collective-permute-start.8
  186.0 40.2 %all_gather.25 = bf16[32,16,128]{2,0,1:T(8,128)(2,1)} all-gather(bf16[32,1,128]{2,0,1:T(8,128)(2,1)S(1)} %get-tuple-element.115), channel_id=1, replica_groups=mesh['seg'=16,'samp'=2] {'seg'}, dimensions={1}, use_global_device_ids=true | all-gather | bytes 139264 | tf_op jit(solution)/shard_map/all_gather | solution.py:27
  226.3 1.5 gather_fusion.4
  228.4 1.9 collective-permute-start.9
  230.5 5.3 %collective-permute-done.9 = bf16[32,1,128]{2,0,1:T(8,128)(2,1)S(1)} collective-permute-done((bf16[32,1,128]{2,0,1:T(8,128)(2,1)S(1)}, bf16[32,1,128]{2,0,1:T(8,128)(2,1)S(1)}, u32[]{:S(2)}, u32[]{:S(2)}) %collective-permute-start.9) | collective-permute-done | bytes 8224 | tf_op jit(solution)/shard_map/ppermute | solution.py:13
  237.8 1.5 fusion.136
  242.5 1.9 collective-permute-start.10
  244.4 40.1 %all_gather.26 = bf16[32,16,128]{2,0,1:T(8,128)(2,1)} all-gather(bf16[32,1,128]{2,0,1:T(8,128)(2,1)S(1)} %get-tuple-element.112), channel_id=1, replica_groups=mesh['seg'=16,'samp'=2] {'seg'}, dimensions={1}, use_global_device_ids=true | all-gather | bytes 139264 | tf_op jit(solution)/shard_map/all_gather | solution.py:27
  284.5 1.5 gather_fusion.5
  286.6 2.1 collective-permute-start.11
  288.9 5.0 %collective-permute-done.11 = bf16[32,1,128]{2,0,1:T(8,128)(2,1)S(1)} collective-permute-done((bf16[32,1,128]{2,0,1:T(8,128)(2,1)S(1)}, bf16[32,1,128]{2,0,1:T(8,128)(2,1)S(1)}, u32[]{:S(2)}, u32[]{:S(2)}) %collective-permute-start.11) | collective-permute-done | bytes 8224 | tf_op jit(solution)/shard_map/ppermute | solution.py:13
  296.0 1.6 fusion.137
  299.8 1.5 fusion.145
  301.9 1.9 collective-permute-start.12
  303.9 40.1 %all_gather.27 = bf16[32,16,128]{2,0,1:T(8,128)(2,1)} all-gather(bf16[32,1,128]{2,0,1:T(8,128)(2,1)S(1)} %get-tuple-element.109), channel_id=1, replica_groups=mesh['seg'=16,'samp'=2] {'seg'}, dimensions={1}, use_global_device_ids=true | all-gather | bytes 139264 | tf_op jit(solution)/shard_map/all_gather | solution.py:27
  344.0 1.5 gather_fusion.6
  346.1 2.0 collective-permute-start.13
  348.2 5.2 %collective-permute-done.13 = bf16[32,1,128]{2,0,1:T(8,128)(2,1)S(1)} collective-permute-done((bf16[32,1,128]{2,0,1:T(8,128)(2,1)S(1)}, bf16[32,1,128]{2,0,1:T(8,128)(2,1)S(1)}, u32[]{:S(2)}, u32[]{:S(2)}) %collective-permute-start.13) | collective-permute-done | bytes 8224 | tf_op jit(solution)/shard_map/ppermute | solution.py:13
  355.5 1.5 fusion.138
  359.6 1.9 collective-permute-start.14
  361.5 37.3 %all_gather.28 = bf16[32,16,128]{2,0,1:T(8,128)(2,1)S(1)} all-gather(bf16[32,1,128]{2,0,1:T(8,128)(2,1)S(1)} %get-tuple-element.106), channel_id=1, replica_groups=mesh['seg'=16,'samp'=2] {'seg'}, dimensions={1}, use_global_device_ids=true | all-gather | bytes 139264 | tf_op jit(solution)/shard_map/all_gather | solution.py:27
  400.1 2.0 collective-permute-start.15
  402.2 5.2 %collective-permute-done.15 = bf16[32,1,128]{2,0,1:T(8,128)(2,1)S(1)} collective-permute-done((bf16[32,1,128]{2,0,1:T(8,128)(2,1)S(1)}, bf16[32,1,128]{2,0,1:T(8,128)(2,1)S(1)}, u32[]{:S(2)}, u32[]{:S(2)}) %collective-permute-start.15) | collective-permute-done | bytes 8224 | tf_op jit(solution)/shard_map/ppermute | solution.py:13
  412.1 48.0 %psum.34 = f32[512]{0:T(512)S(1)} all-reduce(f32[512]{0:T(512)S(1)} %add_add_fusion), channel_id=1, replica_groups=mesh['seg'=16,'samp'=2] {'seg','samp'}, use_global_device_ids=true, to_apply=%region_9.11 | all-reduce | flops 512 | bytes 4096 | tf_op jit(solution)/shard_map/psum | solution.py:126
  (210 shorter events, 47.5 us)
Async XLA Ops:
  0.6 7.8 %copy-start.1 = (bf16[32,128,128]{2,1,0:T(8,128)(2,1)S(1)}, bf16[32,128,128]{2,1,0:T(8,128)(2,1)}, u32[]{:S(2)}) copy-start(bf16[32,128,128]{2,1,0:T(8,128)(2,1)} %param.28) | copy-start | bytes 3145732
  0.7 10.2 %collective-permute-start = (bf16[32,1,128]{2,0,1:T(8,128)(2,1)S(1)}, bf16[32,1,128]{2,0,1:T(8,128)(2,1)S(1)}, u32[]{:S(2)}, u32[]{:S(2)}) collective-permute-start(bf16[32,1,128]{2,0,1:T(8,128)(2,1)S(1)} %slice.302), channel_id=1, source_target_pairs={{0,2},{2,4},{4,6},{6,8},{8,10},{10,12},{12,14},{14,16},{16,18},{18... | collective-permute-start | bytes 24584 | tf_op jit(solution)/shard_map/ppermute | solution.py:13
  4.6 3.9 copy-start.26
  4.6 7.5 %collective-permute-start.1 = (bf16[32,1,128]{2,0,1:T(8,128)(2,1)S(1)}, bf16[32,1,128]{2,0,1:T(8,128)(2,1)S(1)}, u32[]{:S(2)}, u32[]{:S(2)}) collective-permute-start(bf16[32,1,128]{2,0,1:T(8,128)(2,1)S(1)} %slice.366), channel_id=1, source_target_pairs={{2,0},{4,2},{6,4},{8,6},{10,8},{12,10},{14,12},{16,14},{18,16},{20... | collective-permute-start | bytes 24584 | tf_op jit(solution)/shard_map/ppermute | solution.py:13
  14.3 44.7 %copy-start.7 = (bf16[32,32,128]{2,0,1:T(8,128)(2,1)}, bf16[32,32,128]{2,0,1:T(8,128)(2,1)S(1)}, u32[]{:S(2)}) copy-start(bf16[32,32,128]{2,0,1:T(8,128)(2,1)S(1)} %convert_bitcast_fusion) | copy-start | bytes 786436
  17.6 41.5 %collective-permute-start.2 = (bf16[32,1,128]{2,0,1:T(8,128)(2,1)}, bf16[32,1,128]{2,0,1:T(8,128)(2,1)}, u32[]{:S(2)}, u32[]{:S(2)}) collective-permute-start(bf16[32,1,128]{2,0,1:T(8,128)(2,1)} %get-tuple-element.125), channel_id=1, source_target_pairs={{0,2},{2,4},{4,6},{6,8},{8,10},{10,12},{12,14},{14,16},{16,18},{18... | collective-permute-start | bytes 24584 | tf_op jit(solution)/shard_map/ppermute | solution.py:13
  55.5 7.7 %collective-permute-start.3 = (bf16[32,1,128]{2,0,1:T(8,128)(2,1)S(1)}, bf16[32,1,128]{2,0,1:T(8,128)(2,1)S(1)}, u32[]{:S(2)}, u32[]{:S(2)}) collective-permute-start(bf16[32,1,128]{2,0,1:T(8,128)(2,1)S(1)} %slice.371), channel_id=1, source_target_pairs={{2,0},{4,2},{6,4},{8,6},{10,8},{12,10},{14,12},{16,14},{18,16},{20... | collective-permute-start | bytes 24584 | tf_op jit(solution)/shard_map/ppermute | solution.py:13
  59.0 4.2 copy-start.13
  59.1 4.1 slice-start
  59.1 4.1 slice-start.5
  59.1 5.5 %copy-start.4 = (f32[32,32,128]{2,0,1:T(8,128)S(1)}, f32[32,32,128]{2,0,1:T(8,128)}, u32[]{:S(2)}) copy-start(f32[32,32,128]{2,0,1:T(8,128)} %copy-done.3) | copy-start | bytes 1572868
  59.1 5.5 %copy-start.6 = (f32[32,32,128]{2,1,0:T(8,128)S(1)}, f32[32,32,128]{2,1,0:T(8,128)}, u32[]{:S(2)}) copy-start(f32[32,32,128]{2,1,0:T(8,128)} %copy-done.5) | copy-start | bytes 1572868
  69.9 42.7 %collective-permute-start.4 = (bf16[32,1,128]{2,0,1:T(8,128)(2,1)}, bf16[32,1,128]{2,0,1:T(8,128)(2,1)}, u32[]{:S(2)}, u32[]{:S(2)}) collective-permute-start(bf16[32,1,128]{2,0,1:T(8,128)(2,1)} %get-tuple-element.122), channel_id=1, source_target_pairs={{0,2},{2,4},{4,6},{6,8},{8,10},{10,12},{12,14},{14,16},{16,18},{18... | collective-permute-start | bytes 24584 | tf_op jit(solution)/shard_map/ppermute | solution.py:13
  110.5 7.3 %collective-permute-start.5 = (bf16[32,1,128]{2,0,1:T(8,128)(2,1)S(1)}, bf16[32,1,128]{2,0,1:T(8,128)(2,1)S(1)}, u32[]{:S(2)}, u32[]{:S(2)}) collective-permute-start(bf16[32,1,128]{2,0,1:T(8,128)(2,1)S(1)} %slice.377), channel_id=1, source_target_pairs={{2,0},{4,2},{6,4},{8,6},{10,8},{12,10},{14,12},{16,14},{18,16},{20... | collective-permute-start | bytes 24584 | tf_op jit(solution)/shard_map/ppermute | solution.py:13
  112.4 5.4 %copy-start.9 = (f32[32,32,128]{2,1,0:T(8,128)S(1)}, f32[32,32,128]{2,1,0:T(8,128)}, u32[]{:S(2)}) copy-start(f32[32,32,128]{2,1,0:T(8,128)} %fusion.141) | copy-start | bytes 1572868
  112.6 5.3 %slice-start.1 = ((bf16[32,32,128]{2,0,1:T(8,128)(2,1)}), bf16[32,31,128]{2,0,1:T(8,128)(2,1)S(1)}, s32[]{:S(2)}) async-start(bf16[32,32,128]{2,0,1:T(8,128)(2,1)} %fusion.26), calls=%async_computation.1 | async-start | bytes 507904 | tf_op jit(solution)/shard_map/slice | solution.py:32
  112.6 6.7 %copy-start.24 = (f32[32,32,128]{2,0,1:T(8,128)S(1)}, f32[32,32,128]{2,0,1:T(8,128)}, u32[]{:S(2)}) copy-start(f32[32,32,128]{2,0,1:T(8,128)} %get-tuple-element.129) | copy-start | bytes 1572868
  124.6 46.3 %collective-permute-start.6 = (bf16[32,1,128]{2,0,1:T(8,128)(2,1)}, bf16[32,1,128]{2,0,1:T(8,128)(2,1)}, u32[]{:S(2)}, u32[]{:S(2)}) collective-permute-start(bf16[32,1,128]{2,0,1:T(8,128)(2,1)} %get-tuple-element.119), channel_id=1, source_target_pairs={{0,2},{2,4},{4,6},{6,8},{8,10},{10,12},{12,14},{14,16},{16,18},{18... | collective-permute-start | bytes 24584 | tf_op jit(solution)/shard_map/ppermute | solution.py:13
  168.8 7.3 %collective-permute-start.7 = (bf16[32,1,128]{2,0,1:T(8,128)(2,1)S(1)}, bf16[32,1,128]{2,0,1:T(8,128)(2,1)S(1)}, u32[]{:S(2)}, u32[]{:S(2)}) collective-permute-start(bf16[32,1,128]{2,0,1:T(8,128)(2,1)S(1)} %slice.383), channel_id=1, source_target_pairs={{2,0},{4,2},{6,4},{8,6},{10,8},{12,10},{14,12},{16,14},{18,16},{20... | collective-permute-start | bytes 24584 | tf_op jit(solution)/shard_map/ppermute | solution.py:13
  170.7 5.4 %copy-start.14 = (f32[32,32,128]{2,1,0:T(8,128)S(1)}, f32[32,32,128]{2,1,0:T(8,128)}, u32[]{:S(2)}) copy-start(f32[32,32,128]{2,1,0:T(8,128)} %fusion.142) | copy-start | bytes 1572868
  170.8 5.3 %slice-start.6 = ((bf16[32,32,128]{2,0,1:T(8,128)(2,1)}), bf16[32,31,128]{2,0,1:T(8,128)(2,1)S(1)}, s32[]{:S(2)}) async-start(bf16[32,32,128]{2,0,1:T(8,128)(2,1)} %fusion.27), calls=%async_computation.6 | async-start | bytes 507904 | tf_op jit(solution)/shard_map/slice | solution.py:32
  170.8 6.7 %copy-start.19 = (f32[32,32,128]{2,0,1:T(8,128)S(1)}, f32[32,32,128]{2,0,1:T(8,128)}, u32[]{:S(2)}) copy-start(f32[32,32,128]{2,0,1:T(8,128)} %copy-done.18) | copy-start | bytes 1572868
  170.9 6.7 %copy-start.25 = (f32[32,32,128]{2,0,1:T(8,128)S(1)}, f32[32,32,128]{2,0,1:T(8,128)}, u32[]{:S(2)}) copy-start(f32[32,32,128]{2,0,1:T(8,128)} %get-tuple-element.129) | copy-start | bytes 1572868
  170.9 6.7 %copy-start.50 = (f32[32,32,128]{2,0,1:T(8,128)S(1)}, f32[32,32,128]{2,0,1:T(8,128)}, u32[]{:S(2)}) copy-start(f32[32,32,128]{2,0,1:T(8,128)} %get-tuple-element.131) | copy-start | bytes 1572868
  184.1 46.4 %collective-permute-start.8 = (bf16[32,1,128]{2,0,1:T(8,128)(2,1)}, bf16[32,1,128]{2,0,1:T(8,128)(2,1)}, u32[]{:S(2)}, u32[]{:S(2)}) collective-permute-start(bf16[32,1,128]{2,0,1:T(8,128)(2,1)} %get-tuple-element.116), channel_id=1, source_target_pairs={{0,2},{2,4},{4,6},{6,8},{8,10},{10,12},{12,14},{14,16},{16,18},{18... | collective-permute-start | bytes 24584 | tf_op jit(solution)/shard_map/ppermute | solution.py:13
  228.4 7.3 %collective-permute-start.9 = (bf16[32,1,128]{2,0,1:T(8,128)(2,1)S(1)}, bf16[32,1,128]{2,0,1:T(8,128)(2,1)S(1)}, u32[]{:S(2)}, u32[]{:S(2)}) collective-permute-start(bf16[32,1,128]{2,0,1:T(8,128)(2,1)S(1)} %slice.389), channel_id=1, source_target_pairs={{2,0},{4,2},{6,4},{8,6},{10,8},{12,10},{14,12},{16,14},{18,16},{20... | collective-permute-start | bytes 24584 | tf_op jit(solution)/shard_map/ppermute | solution.py:13
  230.3 5.4 %copy-start.10 = (f32[32,32,128]{2,1,0:T(8,128)S(1)}, f32[32,32,128]{2,1,0:T(8,128)}, u32[]{:S(2)}) copy-start(f32[32,32,128]{2,1,0:T(8,128)} %fusion.143) | copy-start | bytes 1572868
  230.5 5.3 %slice-start.2 = ((bf16[32,32,128]{2,0,1:T(8,128)(2,1)}), bf16[32,31,128]{2,0,1:T(8,128)(2,1)S(1)}, s32[]{:S(2)}) async-start(bf16[32,32,128]{2,0,1:T(8,128)(2,1)} %fusion.28), calls=%async_computation.2 | async-start | bytes 507904 | tf_op jit(solution)/shard_map/slice | solution.py:32
  230.5 6.7 %copy-start.47 = (f32[32,32,128]{2,0,1:T(8,128)S(1)}, f32[32,32,128]{2,0,1:T(8,128)}, u32[]{:S(2)}) copy-start(f32[32,32,128]{2,0,1:T(8,128)} %get-tuple-element.133) | copy-start | bytes 1572868
  242.5 46.4 %collective-permute-start.10 = (bf16[32,1,128]{2,0,1:T(8,128)(2,1)}, bf16[32,1,128]{2,0,1:T(8,128)(2,1)}, u32[]{:S(2)}, u32[]{:S(2)}) collective-permute-start(bf16[32,1,128]{2,0,1:T(8,128)(2,1)} %get-tuple-element.113), channel_id=1, source_target_pairs={{0,2},{2,4},{4,6},{6,8},{8,10},{10,12},{12,14},{14,16},{16,18},{18... | collective-permute-start | bytes 24584 | tf_op jit(solution)/shard_map/ppermute | solution.py:13
  286.6 7.3 %collective-permute-start.11 = (bf16[32,1,128]{2,0,1:T(8,128)(2,1)S(1)}, bf16[32,1,128]{2,0,1:T(8,128)(2,1)S(1)}, u32[]{:S(2)}, u32[]{:S(2)}) collective-permute-start(bf16[32,1,128]{2,0,1:T(8,128)(2,1)S(1)} %slice.395), channel_id=1, source_target_pairs={{2,0},{4,2},{6,4},{8,6},{10,8},{12,10},{14,12},{16,14},{18,16},{20... | collective-permute-start | bytes 24584 | tf_op jit(solution)/shard_map/ppermute | solution.py:13
  288.8 5.2 %copy-start.15 = (f32[32,32,128]{2,1,0:T(8,128)S(1)}, f32[32,32,128]{2,1,0:T(8,128)}, u32[]{:S(2)}) copy-start(f32[32,32,128]{2,1,0:T(8,128)} %fusion.144) | copy-start | bytes 1572868
  288.9 5.1 %slice-start.7 = ((bf16[32,32,128]{2,0,1:T(8,128)(2,1)}), bf16[32,31,128]{2,0,1:T(8,128)(2,1)S(1)}, s32[]{:S(2)}) async-start(bf16[32,32,128]{2,0,1:T(8,128)(2,1)} %fusion.29), calls=%async_computation.7 | async-start | bytes 507904 | tf_op jit(solution)/shard_map/slice | solution.py:32
  288.9 6.5 %copy-start.21 = (f32[32,32,128]{2,0,1:T(8,128)S(1)}, f32[32,32,128]{2,0,1:T(8,128)}, u32[]{:S(2)}) copy-start(f32[32,32,128]{2,0,1:T(8,128)} %copy-done.20) | copy-start | bytes 1572868
  288.9 6.5 %copy-start.48 = (f32[32,32,128]{2,0,1:T(8,128)S(1)}, f32[32,32,128]{2,0,1:T(8,128)}, u32[]{:S(2)}) copy-start(f32[32,32,128]{2,0,1:T(8,128)} %get-tuple-element.133) | copy-start | bytes 1572868
  288.9 6.5 %copy-start.51 = (f32[32,32,128]{2,0,1:T(8,128)S(1)}, f32[32,32,128]{2,0,1:T(8,128)}, u32[]{:S(2)}) copy-start(f32[32,32,128]{2,0,1:T(8,128)} %get-tuple-element.135) | copy-start | bytes 1572868
  301.9 46.3 %collective-permute-start.12 = (bf16[32,1,128]{2,0,1:T(8,128)(2,1)}, bf16[32,1,128]{2,0,1:T(8,128)(2,1)}, u32[]{:S(2)}, u32[]{:S(2)}) collective-permute-start(bf16[32,1,128]{2,0,1:T(8,128)(2,1)} %get-tuple-element.110), channel_id=1, source_target_pairs={{0,2},{2,4},{4,6},{6,8},{8,10},{10,12},{12,14},{14,16},{16,18},{18... | collective-permute-start | bytes 24584 | tf_op jit(solution)/shard_map/ppermute | solution.py:13
  346.1 7.3 %collective-permute-start.13 = (bf16[32,1,128]{2,0,1:T(8,128)(2,1)S(1)}, bf16[32,1,128]{2,0,1:T(8,128)(2,1)S(1)}, u32[]{:S(2)}, u32[]{:S(2)}) collective-permute-start(bf16[32,1,128]{2,0,1:T(8,128)(2,1)S(1)} %slice.401), channel_id=1, source_target_pairs={{2,0},{4,2},{6,4},{8,6},{10,8},{12,10},{14,12},{16,14},{18,16},{20... | collective-permute-start | bytes 24584 | tf_op jit(solution)/shard_map/ppermute | solution.py:13
  348.1 5.4 %copy-start.11 = (f32[32,32,128]{2,1,0:T(8,128)S(1)}, f32[32,32,128]{2,1,0:T(8,128)}, u32[]{:S(2)}) copy-start(f32[32,32,128]{2,1,0:T(8,128)} %fusion.145) | copy-start | bytes 1572868
  348.2 5.3 %slice-start.3 = ((bf16[32,32,128]{2,0,1:T(8,128)(2,1)}), bf16[32,31,128]{2,0,1:T(8,128)(2,1)S(1)}, s32[]{:S(2)}) async-start(bf16[32,32,128]{2,0,1:T(8,128)(2,1)} %fusion.30), calls=%async_computation.3 | async-start | bytes 507904 | tf_op jit(solution)/shard_map/slice | solution.py:32
  348.2 6.7 %copy-start.45 = (f32[32,32,128]{2,0,1:T(8,128)S(1)}, f32[32,32,128]{2,0,1:T(8,128)}, u32[]{:S(2)}) copy-start(f32[32,32,128]{2,0,1:T(8,128)} %get-tuple-element.137) | copy-start | bytes 1572868
  359.6 42.6 %collective-permute-start.14 = (bf16[32,1,128]{2,0,1:T(8,128)(2,1)S(1)}, bf16[32,1,128]{2,0,1:T(8,128)(2,1)S(1)}, u32[]{:S(2)}, u32[]{:S(2)}) collective-permute-start(bf16[32,1,128]{2,0,1:T(8,128)(2,1)S(1)} %get-tuple-element.107), channel_id=1, source_target_pairs={{0,2},{2,4},{4,6},{6,8},{8,10},{10,12},{12,14},{14,16},{16,18},{18... | collective-permute-start | bytes 24584 | tf_op jit(solution)/shard_map/ppermute | solution.py:13
  400.1 7.3 %collective-permute-start.15 = (bf16[32,1,128]{2,0,1:T(8,128)(2,1)S(1)}, bf16[32,1,128]{2,0,1:T(8,128)(2,1)S(1)}, u32[]{:S(2)}, u32[]{:S(2)}) collective-permute-start(bf16[32,1,128]{2,0,1:T(8,128)(2,1)S(1)} %slice.407), channel_id=1, source_target_pairs={{2,0},{4,2},{6,4},{8,6},{10,8},{12,10},{14,12},{16,14},{18,16},{20... | collective-permute-start | bytes 24584 | tf_op jit(solution)/shard_map/ppermute | solution.py:13
  402.1 5.3 %copy-start.12 = (f32[32,32,128]{2,1,0:T(8,128)S(1)}, f32[32,32,128]{2,1,0:T(8,128)}, u32[]{:S(2)}) copy-start(f32[32,32,128]{2,1,0:T(8,128)} %fusion.146) | copy-start | bytes 1572868
  402.2 5.2 %slice-start.4 = ((bf16[32,32,128]{2,0,1:T(8,128)(2,1)}), bf16[32,31,128]{2,0,1:T(8,128)(2,1)S(1)}, s32[]{:S(2)}) async-start(bf16[32,32,128]{2,0,1:T(8,128)(2,1)} %fusion.31), calls=%async_computation.4 | async-start | bytes 507904 | tf_op jit(solution)/shard_map/slice | solution.py:32
  402.2 5.9 %copy-start.23 = (f32[32,32,128]{2,0,1:T(8,128)S(1)}, f32[32,32,128]{2,0,1:T(8,128)}, u32[]{:S(2)}) copy-start(f32[32,32,128]{2,0,1:T(8,128)} %copy-done.22) | copy-start | bytes 1572868
  402.2 5.9 %copy-start.46 = (f32[32,32,128]{2,0,1:T(8,128)S(1)}, f32[32,32,128]{2,0,1:T(8,128)}, u32[]{:S(2)}) copy-start(f32[32,32,128]{2,0,1:T(8,128)} %get-tuple-element.137) | copy-start | bytes 1572868
  402.2 5.9 %copy-start.49 = (f32[32,32,128]{2,0,1:T(8,128)S(1)}, f32[32,32,128]{2,0,1:T(8,128)}, u32[]{:S(2)}) copy-start(f32[32,32,128]{2,0,1:T(8,128)} %get-tuple-element.139) | copy-start | bytes 1572868
  (28 other events, 33.2 us)
where the time goes:
time: 462 us; the launch traced here: 461 us
  blocking collectives  311 us (67%)
  matrix products  43.6 us (9%)
  starting transfers between devices  39.7 us (9%)
  waiting for transfers between devices  36.5 us (8%)
  local copies, waits for them, and re-layouts  22.3 us (5%)
  other arithmetic  5.63 us (1%)
    all_gather x7, blocking collectives, stiffness(): lax.all_gather(field_round[:, :1, :], 'seg', axis=1, tiled=True)  263 us
    psum x1, blocking collectives, body(): grad_total = grad_total + lax.psum(partial_value, ('seg', 'samp'))  48 us
    ppermute x16, starting transfers between devices, shifted(): lax.ppermute(value, axis, [(source, source + steps) for source in range(f...  39.7 us
    ppermute x16, waiting for transfers between devices, shifted(): lax.ppermute(value, axis, [(source, source + steps) for source in range(f...  36.5 us
    dot_general x8, matrix products, stiffness(): jnp.einsum('sjb,jab->sja', field_round, rigidity_diagonal_cells, preferre...  11.7 us
    dot_general x8, matrix products, blockwise(): jnp.einsum('jab,sjb->sja', inverse_diagonal_cells, field_round, preferred...  10.8 us
    gather x8, local copies, waits for them, and re-layouts, stiffness(): jnp.take(interfaces, joined_segment_table[0], axis=1).astype(jnp.float32)  9.89 us
    dot_general x8, matrix products, stiffness(): jnp.einsum('sjb,jab->sja', lower_field, rigidity_lower_cells, preferred_e...  9.37 us
  transfers between devices with their start and end apart: 16, of which 8 were waited for; matrix products, arithmetic and copies ran while one was open for 4% of the time, Pallas kernels for 0%

commit v1 on v0

--- a/solution.py
+++ b/solution.py
@@ -24,7 +24,17 @@
     ).astype(jnp.bfloat16)
     below_rim = shifted(field_round[:, -1:, :], "seg", 1)
     above_rim = shifted(upward[:, :1, :], "seg", -1)
-    interfaces = lax.all_gather(field_round[:, :1, :], "seg", axis=1, tiled=True)
+    x = field_round[:, :1, :]
+    ways = lax.axis_size("seg")
+    up = [(d, (d + 1) % ways) for d in range(ways)]
+    down = [(d, (d - 1) % ways) for d in range(ways)]
+    earlier, later = ([x], [x])
+    for _ in range(ways // 2):
+        earlier.append(lax.ppermute(earlier[-1], "seg", up))
+    for _ in range((ways - 1) // 2):
+        later.append(lax.ppermute(later[-1], "seg", down))
+    line = jnp.concatenate([*earlier[::-1], *later[1:]], axis=1)
+    interfaces = jnp.roll(line, (lax.axis_index("seg") - ways // 2) * x.shape[1], axis=1)
     lower_field = jnp.concatenate([below_rim, field_round[:, :-1]], axis=1)
     below_term = jnp.einsum(
         "sjb,jab->sja", lower_field, rigidity_lower_cells, preferred_element_type=jnp.float32

time: 462 us -> 596 us (1.29)
  starting transfers between devices: 39.7 us -> 315 us
  blocking collectives: 311 us -> 58.2 us
  waiting for transfers between devices: 36.5 us -> 129 us
  local copies, waits for them, and re-layouts: 22.3 us -> 34.3 us
  other arithmetic: 5.63 us -> 12.4 us
    all_gather x7 -> x0, blocking collectives: 263 us -> none  [stiffness(): lax.all_gather(field_round[:, :1, :], 'seg', axis=1, tiled=True)]
    ppermute x0 -> x120, starting transfers between devices: none -> 259 us  [the longest x56 198 us: stiffness(): later.append(lax.ppermute(later[-1], 'seg', down))]
    ppermute x0 -> x120, waiting for transfers between devices: none -> 103 us  [the longest x64 100 us: stiffness(): earlier.append(lax.ppermute(earlier[-1], 'seg', up))]
    ppermute x16, starting transfers between devices: 39.7 us -> 55.9 us  [shifted(): lax.ppermute(value, axis, [(source, source + steps) for source in range(f...]
    ppermute x16, waiting for transfers between devices: 36.5 us -> 25.6 us  [shifted(): lax.ppermute(value, axis, [(source, source + steps) for source in range(f...]
    psum x1, blocking collectives: 48 us -> 58.2 us  [body(): grad_total = grad_total + lax.psum(partial_value, ('seg', 'samp'))]
  transfers between devices with their start and end apart: 16 -> 136, of which waited for: 8 -> 68; matrix products, arithmetic and copies ran while one was open for 4% -> 9% of each run, Pallas kernels for 0% -> 0%
where the time goes in v1:
time: 596 us; the launch traced here: 594 us
  starting transfers between devices  315 us (53%)
  waiting for transfers between devices  129 us (22%)
  blocking collectives  58.2 us (10%)
  matrix products  43.2 us (7%)
  local copies, waits for them, and re-layouts  34.3 us (6%)
  other arithmetic  12.4 us (2%)
    ppermute x56, starting transfers between devices, stiffness(): later.append(lax.ppermute(later[-1], 'seg', down))  198 us
    ppermute x64, waiting for transfers between devices, stiffness(): earlier.append(lax.ppermute(earlier[-1], 'seg', up))  100 us
    ppermute x64, starting transfers between devices, stiffness(): earlier.append(lax.ppermute(earlier[-1], 'seg', up))  61 us
    psum x1, blocking collectives, body(): grad_total = grad_total + lax.psum(partial_value, ('seg', 'samp'))  58.2 us
    ppermute x16, starting transfers between devices, shifted(): lax.ppermute(value, axis, [(source, source + steps) for source in range(f...  55.9 us
    ppermute x16, waiting for transfers between devices, shifted(): lax.ppermute(value, axis, [(source, source + steps) for source in range(f...  25.6 us
    dot_general x8, matrix products, stiffness(): jnp.einsum('sjb,jab->sja', lower_field, rigidity_lower_cells, preferred_e...  14.1 us
  transfers between devices with their start and end apart: 136, of which 68 were waited for; matrix products, arithmetic and copies ran while one was open for 9% of the time, Pallas kernels for 0%

profile of v1, /device:TPU:14, one launch (start us, length us, event | category | flops | bytes accessed | tf_op | source)
XLA Modules:
  0.0 593.7 jit_solution(3332813545086737417)
XLA Ops:
  8.0 4.0 collective-permute-start.1
  20.7 4.1 collective-permute-start.5
  26.2 4.1 collective-permute-start.6
  31.7 4.1 collective-permute-start.7
  37.1 4.2 collective-permute-start.8
  42.9 4.2 collective-permute-start.9
  63.7 4.1 collective-permute-start.20
  69.2 4.1 collective-permute-start.21
  74.6 4.1 collective-permute-start.22
  80.1 4.1 collective-permute-start.23
  85.5 4.1 collective-permute-start.24
  91.0 4.1 collective-permute-start.25
  96.5 4.0 collective-permute-start.26
  104.1 4.7 collective-permute-start.33
  114.0 5.0 collective-permute-done.17
  122.4 7.2 %collective-permute-done.36 = bf16[32,1,128]{2,0,1:T(8,128)(2,1)S(1)} collective-permute-done((bf16[32,1,128]{2,0,1:T(8,128)(2,1)S(1)}, bf16[32,1,128]{2,0,1:T(8,128)(2,1)S(1)}, u32[]{:S(2)}, u32[]{:S(2)}) %collective-permute-start.36) | collective-permute-done | bytes 8224 | tf_op jit(solution)/shard_map/ppermute | solution.py:33
  129.7 5.6 collective-permute-start.44
  136.9 5.7 collective-permute-start.45
  144.2 5.6 collective-permute-start.46
  170.2 5.7 collective-permute-start.35
  192.1 6.9 %collective-permute-done.53 = bf16[32,1,128]{2,0,1:T(8,128)(2,1)S(1)} collective-permute-done((bf16[32,1,128]{2,0,1:T(8,128)(2,1)S(1)}, bf16[32,1,128]{2,0,1:T(8,128)(2,1)S(1)}, u32[]{:S(2)}, u32[]{:S(2)}) %collective-permute-start.53) | collective-permute-done | bytes 8224 | tf_op jit(solution)/shard_map/ppermute | solution.py:33
  199.0 5.6 collective-permute-start.61
  206.2 5.6 collective-permute-start.62
  213.4 5.6 collective-permute-start.63
  239.5 5.7 collective-permute-start.52
  261.4 6.2 %collective-permute-done.70 = bf16[32,1,128]{2,0,1:T(8,128)(2,1)S(1)} collective-permute-done((bf16[32,1,128]{2,0,1:T(8,128)(2,1)S(1)}, bf16[32,1,128]{2,0,1:T(8,128)(2,1)S(1)}, u32[]{:S(2)}, u32[]{:S(2)}) %collective-permute-start.70) | collective-permute-done | bytes 8224 | tf_op jit(solution)/shard_map/ppermute | solution.py:33
  267.6 5.7 collective-permute-start.78
  274.9 5.5 collective-permute-start.79
  282.1 5.6 collective-permute-start.80
  308.1 5.7 collective-permute-start.69
  330.0 6.3 %collective-permute-done.87 = bf16[32,1,128]{2,0,1:T(8,128)(2,1)S(1)} collective-permute-done((bf16[32,1,128]{2,0,1:T(8,128)(2,1)S(1)}, bf16[32,1,128]{2,0,1:T(8,128)(2,1)S(1)}, u32[]{:S(2)}, u32[]{:S(2)}) %collective-permute-start.87) | collective-permute-done | bytes 8224 | tf_op jit(solution)/shard_map/ppermute | solution.py:33
  336.3 5.6 collective-permute-start.95
  343.6 5.6 collective-permute-start.96
  350.8 5.6 collective-permute-start.97
  376.8 5.7 collective-permute-start.86
  382.6 3.9 collective-permute-start.101
  398.8 6.2 %collective-permute-done.104 = bf16[32,1,128]{2,0,1:T(8,128)(2,1)S(1)} collective-permute-done((bf16[32,1,128]{2,0,1:T(8,128)(2,1)S(1)}, bf16[32,1,128]{2,0,1:T(8,128)(2,1)S(1)}, u32[]{:S(2)}, u32[]{:S(2)}) %collective-permute-start.104) | collective-permute-done | bytes 8224 | tf_op jit(solution)/shard_map/ppermute | solution.py:33
  405.0 5.6 collective-permute-start.112
  412.2 5.6 collective-permute-start.113
  419.5 5.6 collective-permute-start.114
  445.5 5.7 collective-permute-start.103
  467.9 5.8 collective-permute-done.121
  473.8 5.6 collective-permute-start.129
  481.5 5.7 collective-permute-start.130
  488.5 5.6 collective-permute-start.131
  512.9 5.8 collective-permute-start.120
  526.2 4.7 collective-permute-done.119
  534.9 58.2 %psum.34 = f32[512]{0:T(512)S(1)} all-reduce(f32[512]{0:T(512)S(1)} %add_add_fusion), channel_id=1, replica_groups=mesh['seg'=16,'samp'=2] {'seg','samp'}, use_global_device_ids=true, to_apply=%region_9.12 | all-reduce | flops 512 | bytes 4096 | tf_op jit(solution)/shard_map/psum | solution.py:136
  (562 shorter events, 287.9 us)
Async XLA Ops:
  1.3 18.2 %collective-permute-start.10 = (bf16[32,1,128]{2,0,1:T(8,128)(2,1)}, bf16[32,1,128]{2,0,1:T(8,128)(2,1)S(1)}, u32[]{:S(2)}, u32[]{:S(2)}) collective-permute-start(bf16[32,1,128]{2,0,1:T(8,128)(2,1)} %slice.300), channel_id=1, source_target_pairs={{0,30},{2,0},{4,2},{6,4},{8,6},{10,8},{12,10},{14,12},{16,14},{18,... | collective-permute-start | bytes 24584 | tf_op jit(solution)/shard_map/ppermute | solution.py:35
  1.8 10.3 %collective-permute-start.2 = (bf16[32,1,128]{2,0,1:T(8,128)(2,1)}, bf16[32,1,128]{2,0,1:T(8,128)(2,1)S(1)}, u32[]{:S(2)}, u32[]{:S(2)}) collective-permute-start(bf16[32,1,128]{2,0,1:T(8,128)(2,1)} %slice.300), channel_id=1, source_target_pairs={{0,2},{2,4},{4,6},{6,8},{8,10},{10,12},{12,14},{14,16},{16,18},{18... | collective-permute-start | bytes 24584 | tf_op jit(solution)/shard_map/ppermute | solution.py:33
  5.1 42.0 %collective-permute-start = (bf16[32,1,128]{2,0,1:T(8,128)(2,1)}, bf16[32,1,128]{2,0,1:T(8,128)(2,1)S(1)}, u32[]{:S(2)}, u32[]{:S(2)}) collective-permute-start(bf16[32,1,128]{2,0,1:T(8,128)(2,1)} %slice.300), channel_id=1, source_target_pairs={{0,2},{2,4},{4,6},{6,8},{8,10},{10,12},{12,14},{14,16},{16,18},{18... | collective-permute-start | bytes 24584 | tf_op jit(solution)/shard_map/ppermute | solution.py:13
  8.0 39.1 %collective-permute-start.1 = (bf16[32,1,128]{2,0,1:T(8,128)(2,1)}, bf16[32,1,128]{2,0,1:T(8,128)(2,1)S(1)}, u32[]{:S(2)}, u32[]{:S(2)}) collective-permute-start(bf16[32,1,128]{2,0,1:T(8,128)(2,1)} %slice.363), channel_id=1, source_target_pairs={{2,0},{4,2},{6,4},{8,6},{10,8},{12,10},{14,12},{16,14},{18,16},{20... | collective-permute-start | bytes 24584 | tf_op jit(solution)/shard_map/ppermute | solution.py:13
  41.8 7.8 %collective-permute-start.15 = (bf16[32,1,128]{2,0,1:T(8,128)(2,1)}, bf16[32,1,128]{2,0,1:T(8,128)(2,1)S(1)}, u32[]{:S(2)}, u32[]{:S(2)}) collective-permute-start(bf16[32,1,128]{2,0,1:T(8,128)(2,1)} %collective-permute-done.14), channel_id=1, source_target_pairs={{0,30},{2,0},{4,2},{6,4},{8,6},{10,8},{12,10},{14,12},{16,14},{18,... | collective-permute-start | bytes 24584 | tf_op jit(solution)/shard_map/ppermute | solution.py:35
  96.5 7.6 %collective-permute-start.32 = (bf16[32,1,128]{2,0,1:T(8,128)(2,1)S(1)}, bf16[32,1,128]{2,0,1:T(8,128)(2,1)S(1)}, u32[]{:S(2)}, u32[]{:S(2)}) collective-permute-start(bf16[32,1,128]{2,0,1:T(8,128)(2,1)S(1)} %collective-permute-done.31), channel_id=1, source_target_pairs={{0,30},{2,0},{4,2},{6,4},{8,6},{10,8},{12,10},{14,12},{16,14},{18,... | collective-permute-start | bytes 24584 | tf_op jit(solution)/shard_map/ppermute | solution.py:35
  96.5 12.3 %collective-permute-start.26 = (bf16[32,1,128]{2,0,1:T(8,128)(2,1)S(1)}, bf16[32,1,128]{2,0,1:T(8,128)(2,1)S(1)}, u32[]{:S(2)}, u32[]{:S(2)}) collective-permute-start(bf16[32,1,128]{2,0,1:T(8,128)(2,1)S(1)} %collective-permute-done.25), channel_id=1, source_target_pairs={{0,2},{2,4},{4,6},{6,8},{8,10},{10,12},{12,14},{14,16},{16,18},{18... | collective-permute-start | bytes 24584 | tf_op jit(solution)/shard_map/ppermute | solution.py:33
  102.2 11.8 %collective-permute-start.18 = (bf16[32,1,128]{2,0,1:T(8,128)(2,1)}, bf16[32,1,128]{2,0,1:T(8,128)(2,1)}, u32[]{:S(2)}, u32[]{:S(2)}) collective-permute-start(bf16[32,1,128]{2,0,1:T(8,128)(2,1)} %slice.368), channel_id=1, source_target_pairs={{2,0},{4,2},{6,4},{8,6},{10,8},{12,10},{14,12},{16,14},{18,16},{20... | collective-permute-start | bytes 24584 | tf_op jit(solution)/shard_map/ppermute | solution.py:13
  104.1 7.5 %collective-permute-start.33 = (bf16[32,1,128]{2,0,1:T(8,128)(2,1)S(1)}, bf16[32,1,128]{2,0,1:T(8,128)(2,1)S(1)}, u32[]{:S(2)}, u32[]{:S(2)}) collective-permute-start(bf16[32,1,128]{2,0,1:T(8,128)(2,1)S(1)} %collective-permute-done.32), channel_id=1, source_target_pairs={{0,30},{2,0},{4,2},{6,4},{8,6},{10,8},{12,10},{14,12},{16,14},{18,... | collective-permute-start | bytes 24584 | tf_op jit(solution)/shard_map/ppermute | solution.py:35
  109.5 9.5 %collective-permute-start.17 = (bf16[32,1,128]{2,0,1:T(8,128)(2,1)}, bf16[32,1,128]{2,0,1:T(8,128)(2,1)S(1)}, u32[]{:S(2)}, u32[]{:S(2)}) collective-permute-start(bf16[32,1,128]{2,0,1:T(8,128)(2,1)} %get-tuple-element.124), channel_id=1, source_target_pairs={{0,2},{2,4},{4,6},{6,8},{8,10},{10,12},{12,14},{14,16},{16,18},{18... | collective-permute-start | bytes 24584 | tf_op jit(solution)/shard_map/ppermute | solution.py:13
  129.7 7.2 %collective-permute-start.44 = (bf16[32,1,128]{2,0,1:T(8,128)(2,1)S(1)}, bf16[32,1,128]{2,0,1:T(8,128)(2,1)S(1)}, u32[]{:S(2)}, u32[]{:S(2)}) collective-permute-start(bf16[32,1,128]{2,0,1:T(8,128)(2,1)S(1)} %slice.376), channel_id=1, source_target_pairs={{0,30},{2,0},{4,2},{6,4},{8,6},{10,8},{12,10},{14,12},{16,14},{18,... | collective-permute-start | bytes 24584 | tf_op jit(solution)/shard_map/ppermute | solution.py:35
  136.9 7.3 %collective-permute-start.38 = (bf16[32,1,128]{2,0,1:T(8,128)(2,1)S(1)}, bf16[32,1,128]{2,0,1:T(8,128)(2,1)S(1)}, u32[]{:S(2)}, u32[]{:S(2)}) collective-permute-start(bf16[32,1,128]{2,0,1:T(8,128)(2,1)S(1)} %collective-permute-done.37), channel_id=1, source_target_pairs={{0,2},{2,4},{4,6},{6,8},{8,10},{10,12},{12,14},{14,16},{16,18},{18... | collective-permute-start | bytes 24584 | tf_op jit(solution)/shard_map/ppermute | solution.py:33
  136.9 7.3 %collective-permute-start.45 = (bf16[32,1,128]{2,0,1:T(8,128)(2,1)S(1)}, bf16[32,1,128]{2,0,1:T(8,128)(2,1)S(1)}, u32[]{:S(2)}, u32[]{:S(2)}) collective-permute-start(bf16[32,1,128]{2,0,1:T(8,128)(2,1)S(1)} %collective-permute-done.44), channel_id=1, source_target_pairs={{0,30},{2,0},{4,2},{6,4},{8,6},{10,8},{12,10},{14,12},{16,14},{18,... | collective-permute-start | bytes 24584 | tf_op jit(solution)/shard_map/ppermute | solution.py:35
  163.8 12.1 %collective-permute-start.49 = (bf16[32,1,128]{2,0,1:T(8,128)(2,1)S(1)}, bf16[32,1,128]{2,0,1:T(8,128)(2,1)S(1)}, u32[]{:S(2)}, u32[]{:S(2)}) collective-permute-start(bf16[32,1,128]{2,0,1:T(8,128)(2,1)S(1)} %collective-permute-done.48), channel_id=1, source_target_pairs={{0,30},{2,0},{4,2},{6,4},{8,6},{10,8},{12,10},{14,12},{16,14},{18,... | collective-permute-start | bytes 24584 | tf_op jit(solution)/shard_map/ppermute | solution.py:35
  167.7 12.0 %collective-permute-start.43 = (bf16[32,1,128]{2,0,1:T(8,128)(2,1)S(1)}, bf16[32,1,128]{2,0,1:T(8,128)(2,1)S(1)}, u32[]{:S(2)}, u32[]{:S(2)}) collective-permute-start(bf16[32,1,128]{2,0,1:T(8,128)(2,1)S(1)} %collective-permute-done.42), channel_id=1, source_target_pairs={{0,2},{2,4},{4,6},{6,8},{8,10},{10,12},{12,14},{14,16},{16,18},{18... | collective-permute-start | bytes 24584 | tf_op jit(solution)/shard_map/ppermute | solution.py:33
  170.2 14.6 %collective-permute-start.35 = (bf16[32,1,128]{2,0,1:T(8,128)(2,1)}, bf16[32,1,128]{2,0,1:T(8,128)(2,1)S(1)}, u32[]{:S(2)}, u32[]{:S(2)}) collective-permute-start(bf16[32,1,128]{2,0,1:T(8,128)(2,1)} %slice.374), channel_id=1, source_target_pairs={{2,0},{4,2},{6,4},{8,6},{10,8},{12,10},{14,12},{16,14},{18,16},{20... | collective-permute-start | bytes 24584 | tf_op jit(solution)/shard_map/ppermute | solution.py:13
  180.5 7.5 %collective-permute-start.34 = (bf16[32,1,128]{2,0,1:T(8,128)(2,1)}, bf16[32,1,128]{2,0,1:T(8,128)(2,1)S(1)}, u32[]{:S(2)}, u32[]{:S(2)}) collective-permute-start(bf16[32,1,128]{2,0,1:T(8,128)(2,1)} %get-tuple-element.121), channel_id=1, source_target_pairs={{0,2},{2,4},{4,6},{6,8},{8,10},{10,12},{12,14},{14,16},{16,18},{18... | collective-permute-start | bytes 24584 | tf_op jit(solution)/shard_map/ppermute | solution.py:13
  213.4 7.3 %collective-permute-start.56 = (bf16[32,1,128]{2,0,1:T(8,128)(2,1)S(1)}, bf16[32,1,128]{2,0,1:T(8,128)(2,1)S(1)}, u32[]{:S(2)}, u32[]{:S(2)}) collective-permute-start(bf16[32,1,128]{2,0,1:T(8,128)(2,1)S(1)} %collective-permute-done.55), channel_id=1, source_target_pairs={{0,2},{2,4},{4,6},{6,8},{8,10},{10,12},{12,14},{14,16},{16,18},{18... | collective-permute-start | bytes 24584 | tf_op jit(solution)/shard_map/ppermute | solution.py:33
  213.4 7.3 %collective-permute-start.63 = (bf16[32,1,128]{2,0,1:T(8,128)(2,1)S(1)}, bf16[32,1,128]{2,0,1:T(8,128)(2,1)S(1)}, u32[]{:S(2)}, u32[]{:S(2)}) collective-permute-start(bf16[32,1,128]{2,0,1:T(8,128)(2,1)S(1)} %collective-permute-done.62), channel_id=1, source_target_pairs={{0,30},{2,0},{4,2},{6,4},{8,6},{10,8},{12,10},{14,12},{16,14},{18,... | collective-permute-start | bytes 24584 | tf_op jit(solution)/shard_map/ppermute | solution.py:35
  233.1 12.1 %collective-permute-start.66 = (bf16[32,1,128]{2,0,1:T(8,128)(2,1)S(1)}, bf16[32,1,128]{2,0,1:T(8,128)(2,1)S(1)}, u32[]{:S(2)}, u32[]{:S(2)}) collective-permute-start(bf16[32,1,128]{2,0,1:T(8,128)(2,1)S(1)} %collective-permute-done.65), channel_id=1, source_target_pairs={{0,30},{2,0},{4,2},{6,4},{8,6},{10,8},{12,10},{14,12},{16,14},{18,... | collective-permute-start | bytes 24584 | tf_op jit(solution)/shard_map/ppermute | solution.py:35
  237.0 12.0 %collective-permute-start.60 = (bf16[32,1,128]{2,0,1:T(8,128)(2,1)S(1)}, bf16[32,1,128]{2,0,1:T(8,128)(2,1)S(1)}, u32[]{:S(2)}, u32[]{:S(2)}) collective-permute-start(bf16[32,1,128]{2,0,1:T(8,128)(2,1)S(1)} %collective-permute-done.59), channel_id=1, source_target_pairs={{0,2},{2,4},{4,6},{6,8},{8,10},{10,12},{12,14},{14,16},{16,18},{18... | collective-permute-start | bytes 24584 | tf_op jit(solution)/shard_map/ppermute | solution.py:33
  239.5 14.6 %collective-permute-start.52 = (bf16[32,1,128]{2,0,1:T(8,128)(2,1)}, bf16[32,1,128]{2,0,1:T(8,128)(2,1)S(1)}, u32[]{:S(2)}, u32[]{:S(2)}) collective-permute-start(bf16[32,1,128]{2,0,1:T(8,128)(2,1)} %slice.380), channel_id=1, source_target_pairs={{2,0},{4,2},{6,4},{8,6},{10,8},{12,10},{14,12},{16,14},{18,16},{20... | collective-permute-start | bytes 24584 | tf_op jit(solution)/shard_map/ppermute | solution.py:13
  249.7 7.6 %collective-permute-start.51 = (bf16[32,1,128]{2,0,1:T(8,128)(2,1)}, bf16[32,1,128]{2,0,1:T(8,128)(2,1)S(1)}, u32[]{:S(2)}, u32[]{:S(2)}) collective-permute-start(bf16[32,1,128]{2,0,1:T(8,128)(2,1)} %get-tuple-element.118), channel_id=1, source_target_pairs={{0,2},{2,4},{4,6},{6,8},{8,10},{10,12},{12,14},{14,16},{16,18},{18... | collective-permute-start | bytes 24584 | tf_op jit(solution)/shard_map/ppermute | solution.py:13
  267.6 7.3 %collective-permute-start.71 = (bf16[32,1,128]{2,0,1:T(8,128)(2,1)S(1)}, bf16[32,1,128]{2,0,1:T(8,128)(2,1)S(1)}, u32[]{:S(2)}, u32[]{:S(2)}) collective-permute-start(bf16[32,1,128]{2,0,1:T(8,128)(2,1)S(1)} %collective-permute-done.70), channel_id=1, source_target_pairs={{0,2},{2,4},{4,6},{6,8},{8,10},{10,12},{12,14},{14,16},{16,18},{18... | collective-permute-start | bytes 24584 | tf_op jit(solution)/shard_map/ppermute | solution.py:33
  267.6 7.3 %collective-permute-start.78 = (bf16[32,1,128]{2,0,1:T(8,128)(2,1)S(1)}, bf16[32,1,128]{2,0,1:T(8,128)(2,1)S(1)}, u32[]{:S(2)}, u32[]{:S(2)}) collective-permute-start(bf16[32,1,128]{2,0,1:T(8,128)(2,1)S(1)} %slice.388), channel_id=1, source_target_pairs={{0,30},{2,0},{4,2},{6,4},{8,6},{10,8},{12,10},{14,12},{16,14},{18,... | collective-permute-start | bytes 24584 | tf_op jit(solution)/shard_map/ppermute | solution.py:35
  301.7 12.1 %collective-permute-start.83 = (bf16[32,1,128]{2,0,1:T(8,128)(2,1)S(1)}, bf16[32,1,128]{2,0,1:T(8,128)(2,1)S(1)}, u32[]{:S(2)}, u32[]{:S(2)}) collective-permute-start(bf16[32,1,128]{2,0,1:T(8,128)(2,1)S(1)} %collective-permute-done.82), channel_id=1, source_target_pairs={{0,30},{2,0},{4,2},{6,4},{8,6},{10,8},{12,10},{14,12},{16,14},{18,... | collective-permute-start | bytes 24584 | tf_op jit(solution)/shard_map/ppermute | solution.py:35
  305.6 12.0 %collective-permute-start.77 = (bf16[32,1,128]{2,0,1:T(8,128)(2,1)S(1)}, bf16[32,1,128]{2,0,1:T(8,128)(2,1)S(1)}, u32[]{:S(2)}, u32[]{:S(2)}) collective-permute-start(bf16[32,1,128]{2,0,1:T(8,128)(2,1)S(1)} %collective-permute-done.76), channel_id=1, source_target_pairs={{0,2},{2,4},{4,6},{6,8},{8,10},{10,12},{12,14},{14,16},{16,18},{18... | collective-permute-start | bytes 24584 | tf_op jit(solution)/shard_map/ppermute | solution.py:33
  308.1 14.6 %collective-permute-start.69 = (bf16[32,1,128]{2,0,1:T(8,128)(2,1)}, bf16[32,1,128]{2,0,1:T(8,128)(2,1)S(1)}, u32[]{:S(2)}, u32[]{:S(2)}) collective-permute-start(bf16[32,1,128]{2,0,1:T(8,128)(2,1)} %slice.386), channel_id=1, source_target_pairs={{2,0},{4,2},{6,4},{8,6},{10,8},{12,10},{14,12},{16,14},{18,16},{20... | collective-permute-start | bytes 24584 | tf_op jit(solution)/shard_map/ppermute | solution.py:13
  318.4 7.5 %collective-permute-start.68 = (bf16[32,1,128]{2,0,1:T(8,128)(2,1)}, bf16[32,1,128]{2,0,1:T(8,128)(2,1)S(1)}, u32[]{:S(2)}, u32[]{:S(2)}) collective-permute-start(bf16[32,1,128]{2,0,1:T(8,128)(2,1)} %get-tuple-element.115), channel_id=1, source_target_pairs={{0,2},{2,4},{4,6},{6,8},{8,10},{10,12},{12,14},{14,16},{16,18},{18... | collective-permute-start | bytes 24584 | tf_op jit(solution)/shard_map/ppermute | solution.py:13
  336.3 7.2 %collective-permute-start.95 = (bf16[32,1,128]{2,0,1:T(8,128)(2,1)S(1)}, bf16[32,1,128]{2,0,1:T(8,128)(2,1)S(1)}, u32[]{:S(2)}, u32[]{:S(2)}) collective-permute-start(bf16[32,1,128]{2,0,1:T(8,128)(2,1)S(1)} %slice.394), channel_id=1, source_target_pairs={{0,30},{2,0},{4,2},{6,4},{8,6},{10,8},{12,10},{14,12},{16,14},{18,... | collective-permute-start | bytes 24584 | tf_op jit(solution)/shard_map/ppermute | solution.py:35
  370.4 12.1 %collective-permute-start.100 = (bf16[32,1,128]{2,0,1:T(8,128)(2,1)S(1)}, bf16[32,1,128]{2,0,1:T(8,128)(2,1)S(1)}, u32[]{:S(2)}, u32[]{:S(2)}) collective-permute-start(bf16[32,1,128]{2,0,1:T(8,128)(2,1)S(1)} %collective-permute-done.99), channel_id=1, source_target_pairs={{0,30},{2,0},{4,2},{6,4},{8,6},{10,8},{12,10},{14,12},{16,14},{18,... | collective-permute-start | bytes 24584 | tf_op jit(solution)/shard_map/ppermute | solution.py:35
  374.4 12.0 %collective-permute-start.94 = (bf16[32,1,128]{2,0,1:T(8,128)(2,1)S(1)}, bf16[32,1,128]{2,0,1:T(8,128)(2,1)S(1)}, u32[]{:S(2)}, u32[]{:S(2)}) collective-permute-start(bf16[32,1,128]{2,0,1:T(8,128)(2,1)S(1)} %collective-permute-done.93), channel_id=1, source_target_pairs={{0,2},{2,4},{4,6},{6,8},{8,10},{10,12},{12,14},{14,16},{16,18},{18... | collective-permute-start | bytes 24584 | tf_op jit(solution)/shard_map/ppermute | solution.py:33
  376.8 14.6 %collective-permute-start.86 = (bf16[32,1,128]{2,0,1:T(8,128)(2,1)}, bf16[32,1,128]{2,0,1:T(8,128)(2,1)S(1)}, u32[]{:S(2)}, u32[]{:S(2)}) collective-permute-start(bf16[32,1,128]{2,0,1:T(8,128)(2,1)} %slice.392), channel_id=1, source_target_pairs={{2,0},{4,2},{6,4},{8,6},{10,8},{12,10},{14,12},{16,14},{18,16},{20... | collective-permute-start | bytes 24584 | tf_op jit(solution)/shard_map/ppermute | solution.py:13
  387.1 7.5 %collective-permute-start.85 = (bf16[32,1,128]{2,0,1:T(8,128)(2,1)}, bf16[32,1,128]{2,0,1:T(8,128)(2,1)S(1)}, u32[]{:S(2)}, u32[]{:S(2)}) collective-permute-start(bf16[32,1,128]{2,0,1:T(8,128)(2,1)} %get-tuple-element.112), channel_id=1, source_target_pairs={{0,2},{2,4},{4,6},{6,8},{8,10},{10,12},{12,14},{14,16},{16,18},{18... | collective-permute-start | bytes 24584 | tf_op jit(solution)/shard_map/ppermute | solution.py:13
  405.0 7.3 %collective-permute-start.105 = (bf16[32,1,128]{2,0,1:T(8,128)(2,1)S(1)}, bf16[32,1,128]{2,0,1:T(8,128)(2,1)S(1)}, u32[]{:S(2)}, u32[]{:S(2)}) collective-permute-start(bf16[32,1,128]{2,0,1:T(8,128)(2,1)S(1)} %collective-permute-done.104), channel_id=1, source_target_pairs={{0,2},{2,4},{4,6},{6,8},{8,10},{10,12},{12,14},{14,16},{16,18},{18... | collective-permute-start | bytes 24584 | tf_op jit(solution)/shard_map/ppermute | solution.py:33
  405.0 7.3 %collective-permute-start.112 = (bf16[32,1,128]{2,0,1:T(8,128)(2,1)S(1)}, bf16[32,1,128]{2,0,1:T(8,128)(2,1)S(1)}, u32[]{:S(2)}, u32[]{:S(2)}) collective-permute-start(bf16[32,1,128]{2,0,1:T(8,128)(2,1)S(1)} %slice.400), channel_id=1, source_target_pairs={{0,30},{2,0},{4,2},{6,4},{8,6},{10,8},{12,10},{14,12},{16,14},{18,... | collective-permute-start | bytes 24584 | tf_op jit(solution)/shard_map/ppermute | solution.py:35
  412.2 7.3 %collective-permute-start.106 = (bf16[32,1,128]{2,0,1:T(8,128)(2,1)S(1)}, bf16[32,1,128]{2,0,1:T(8,128)(2,1)S(1)}, u32[]{:S(2)}, u32[]{:S(2)}) collective-permute-start(bf16[32,1,128]{2,0,1:T(8,128)(2,1)S(1)} %collective-permute-done.105), channel_id=1, source_target_pairs={{0,2},{2,4},{4,6},{6,8},{8,10},{10,12},{12,14},{14,16},{16,18},{18... | collective-permute-start | bytes 24584 | tf_op jit(solution)/shard_map/ppermute | solution.py:33
  412.2 7.3 %collective-permute-start.113 = (bf16[32,1,128]{2,0,1:T(8,128)(2,1)S(1)}, bf16[32,1,128]{2,0,1:T(8,128)(2,1)S(1)}, u32[]{:S(2)}, u32[]{:S(2)}) collective-permute-start(bf16[32,1,128]{2,0,1:T(8,128)(2,1)S(1)} %collective-permute-done.112), channel_id=1, source_target_pairs={{0,30},{2,0},{4,2},{6,4},{8,6},{10,8},{12,10},{14,12},{16,14},{18,... | collective-permute-start | bytes 24584 | tf_op jit(solution)/shard_map/ppermute | solution.py:35
  439.1 12.1 %collective-permute-start.117 = (bf16[32,1,128]{2,0,1:T(8,128)(2,1)S(1)}, bf16[32,1,128]{2,0,1:T(8,128)(2,1)S(1)}, u32[]{:S(2)}, u32[]{:S(2)}) collective-permute-start(bf16[32,1,128]{2,0,1:T(8,128)(2,1)S(1)} %collective-permute-done.116), channel_id=1, source_target_pairs={{0,30},{2,0},{4,2},{6,4},{8,6},{10,8},{12,10},{14,12},{16,14},{18,... | collective-permute-start | bytes 24584 | tf_op jit(solution)/shard_map/ppermute | solution.py:35
  443.1 12.0 %collective-permute-start.111 = (bf16[32,1,128]{2,0,1:T(8,128)(2,1)S(1)}, bf16[32,1,128]{2,0,1:T(8,128)(2,1)S(1)}, u32[]{:S(2)}, u32[]{:S(2)}) collective-permute-start(bf16[32,1,128]{2,0,1:T(8,128)(2,1)S(1)} %collective-permute-done.110), channel_id=1, source_target_pairs={{0,2},{2,4},{4,6},{6,8},{8,10},{10,12},{12,14},{14,16},{16,18},{18... | collective-permute-start | bytes 24584 | tf_op jit(solution)/shard_map/ppermute | solution.py:33
  445.5 14.9 %collective-permute-start.103 = (bf16[32,1,128]{2,0,1:T(8,128)(2,1)}, bf16[32,1,128]{2,0,1:T(8,128)(2,1)S(1)}, u32[]{:S(2)}, u32[]{:S(2)}) collective-permute-start(bf16[32,1,128]{2,0,1:T(8,128)(2,1)} %slice.398), channel_id=1, source_target_pairs={{2,0},{4,2},{6,4},{8,6},{10,8},{12,10},{14,12},{16,14},{18,16},{20... | collective-permute-start | bytes 24584 | tf_op jit(solution)/shard_map/ppermute | solution.py:13
  455.8 7.5 %collective-permute-start.102 = (bf16[32,1,128]{2,0,1:T(8,128)(2,1)}, bf16[32,1,128]{2,0,1:T(8,128)(2,1)S(1)}, u32[]{:S(2)}, u32[]{:S(2)}) collective-permute-start(bf16[32,1,128]{2,0,1:T(8,128)(2,1)} %get-tuple-element.109), channel_id=1, source_target_pairs={{0,2},{2,4},{4,6},{6,8},{8,10},{10,12},{12,14},{14,16},{16,18},{18... | collective-permute-start | bytes 24584 | tf_op jit(solution)/shard_map/ppermute | solution.py:13
  473.8 7.6 %collective-permute-start.129 = (bf16[32,1,128]{2,0,1:T(8,128)(2,1)S(1)}, bf16[32,1,128]{2,0,1:T(8,128)(2,1)S(1)}, u32[]{:S(2)}, u32[]{:S(2)}) collective-permute-start(bf16[32,1,128]{2,0,1:T(8,128)(2,1)S(1)} %slice.406), channel_id=1, source_target_pairs={{0,30},{2,0},{4,2},{6,4},{8,6},{10,8},{12,10},{14,12},{16,14},{18,... | collective-permute-start | bytes 24584 | tf_op jit(solution)/shard_map/ppermute | solution.py:35
  488.5 7.5 %collective-permute-start.131 = (bf16[32,1,128]{2,0,1:T(8,128)(2,1)S(1)}, bf16[32,1,128]{2,0,1:T(8,128)(2,1)S(1)}, u32[]{:S(2)}, u32[]{:S(2)}) collective-permute-start(bf16[32,1,128]{2,0,1:T(8,128)(2,1)S(1)} %collective-permute-done.130), channel_id=1, source_target_pairs={{0,30},{2,0},{4,2},{6,4},{8,6},{10,8},{12,10},{14,12},{16,14},{18,... | collective-permute-start | bytes 24584 | tf_op jit(solution)/shard_map/ppermute | solution.py:35
  507.8 11.0 %collective-permute-start.134 = (bf16[32,1,128]{2,0,1:T(8,128)(2,1)S(1)}, bf16[32,1,128]{2,0,1:T(8,128)(2,1)S(1)}, u32[]{:S(2)}, u32[]{:S(2)}) collective-permute-start(bf16[32,1,128]{2,0,1:T(8,128)(2,1)S(1)} %collective-permute-done.133), channel_id=1, source_target_pairs={{0,30},{2,0},{4,2},{6,4},{8,6},{10,8},{12,10},{14,12},{16,14},{18,... | collective-permute-start | bytes 24584 | tf_op jit(solution)/shard_map/ppermute | solution.py:35
  511.8 10.9 %collective-permute-start.128 = (bf16[32,1,128]{2,0,1:T(8,128)(2,1)S(1)}, bf16[32,1,128]{2,0,1:T(8,128)(2,1)S(1)}, u32[]{:S(2)}, u32[]{:S(2)}) collective-permute-start(bf16[32,1,128]{2,0,1:T(8,128)(2,1)S(1)} %collective-permute-done.127), channel_id=1, source_target_pairs={{0,2},{2,4},{4,6},{6,8},{8,10},{10,12},{12,14},{14,16},{16,18},{18... | collective-permute-start | bytes 24584 | tf_op jit(solution)/shard_map/ppermute | solution.py:33
  512.9 13.2 %collective-permute-start.120 = (bf16[32,1,128]{2,0,1:T(8,128)(2,1)}, bf16[32,1,128]{2,0,1:T(8,128)(2,1)S(1)}, u32[]{:S(2)}, u32[]{:S(2)}) collective-permute-start(bf16[32,1,128]{2,0,1:T(8,128)(2,1)} %slice.404), channel_id=1, source_target_pairs={{2,0},{4,2},{6,4},{8,6},{10,8},{12,10},{14,12},{16,14},{18,16},{20... | collective-permute-start | bytes 24584 | tf_op jit(solution)/shard_map/ppermute | solution.py:13
  523.4 7.5 %collective-permute-start.119 = (bf16[32,1,128]{2,0,1:T(8,128)(2,1)}, bf16[32,1,128]{2,0,1:T(8,128)(2,1)S(1)}, u32[]{:S(2)}, u32[]{:S(2)}) collective-permute-start(bf16[32,1,128]{2,0,1:T(8,128)(2,1)} %get-tuple-element.106), channel_id=1, source_target_pairs={{0,2},{2,4},{4,6},{6,8},{8,10},{10,12},{12,14},{14,16},{16,18},{18... | collective-permute-start | bytes 24584 | tf_op jit(solution)/shard_map/ppermute | solution.py:13
  (137 other events, 1050.6 us)
